TPU v7x, 32 devices: a whole 2x2x4 slice. The times are simulated.
32 devices in a mesh: dp: 4 (over y, x), space: 8 (over z, core).
Axes of the slice: x: 2, y: 2, z: 4, core: 2. Of those that a mesh axis runs over, the one named last changes fastest.
Arguments:
- volumes: bfloat16 [4, 32, 16, 48, 128], P('dp', None, 'space'), may hold values from -6 to 6
- kernel: bfloat16 [3, 3, 3, 64, 32], replicated, may hold values from -0.21875 to 0.21875
- bias: float32 [64], replicated, may hold values from -3 to 3
- cotangent: bfloat16 [4, 64, 16, 48, 128], P('dp', None, 'space'), may hold values from -6 to 6
- finished_grads: float32 [4, 8, 262144], P('dp', 'space'), may hold values from -0.5 to 0.5
Outputs:
- activations: bfloat16 [4, 64, 16, 48, 128], P('dp', None, 'space')
- grad_volumes: bfloat16 [4, 32, 16, 48, 128], P('dp', None, 'space')
- grad_kernel: float32 [3, 3, 3, 64, 32], replicated
- grad_bias: float32 [64], replicated
- summed_grads: float32 [262144], replicated
All inputs are finite; a program needn't handle non-finite values.
Results may differ from a plain program's by a relative error of at most 0.006.
Values may be sent and summed in bfloat16 or wider, within the bound.
A program may use at most 128 MiB of HBM per device.

v0:
```python
import functools
import math

import jax
import jax.numpy as jnp
from jax import lax
from jax.experimental import pallas as pl
from jax.experimental.pallas import tpu as pltpu
from jax.sharding import PartitionSpec as P

VMEM = pl.BlockSpec(memory_space=pltpu.VMEM)
STEP = 2


def spread(block):
    wide = block.astype(jnp.float32)
    columns = wide.shape[1]
    lane = lax.broadcasted_iota(jnp.int32, wide.shape, 1)
    right = jnp.where(lane == 0, 0.0, pltpu.roll(wide, 1, 1))
    left = jnp.where(lane == columns - 1, 0.0, pltpu.roll(wide, columns - 1, 1))
    return right.astype(block.dtype), block, left.astype(block.dtype)


def fill(taps, plane, row, block):
    channels = block.shape[0]
    for k, part in enumerate(spread(block)):
        taps[plane, row + 1, k * channels : (k + 1) * channels, :] = part


def clear_rim(taps):
    planes, rows, depth, columns = taps.shape
    for plane in range(planes):
        for row in (0, rows - 1):
            taps[plane, row] = jnp.zeros((depth, columns), taps.dtype)


def patch(taps, row):
    planes, _, depth, columns = taps.shape
    tall = []
    for plane in range(planes):
        tall.append(
            jnp.concatenate(
                [
                    taps[plane, pl.ds(row + r, 3)].reshape(3 * depth, columns)
                    for r in range(STEP)
                ],
                axis=1,
            )
        )
    return jnp.concatenate(tall, axis=0)


def forward_kernel(lo, mid, hi, w, bias, cot, act, gp, gk, gb, taps):
    depth, rows, channels, columns = mid.shape
    outs = cot.shape[2]
    clear_rim(taps)

    @pl.loop(0, rows)
    def _(row):
        fill(taps, 0, row, lo[row])
        for z in range(depth):
            fill(taps, z + 1, row, mid[z, row])
        fill(taps, depth + 1, row, hi[row])

    gk[...] = jnp.zeros_like(gk)
    gb[...] = jnp.zeros_like(gb)

    @pl.loop(0, rows // STEP)
    def _(step):
        row = step * STEP
        cells = patch(taps, row)
        pre = jnp.dot(w[...], cells, preferred_element_type=jnp.float32) + bias[...]
        grads = []
        for z in range(depth):
            line = []
            for r in range(STEP):
                v = pre[z * outs : (z + 1) * outs, r * columns : (r + 1) * columns]
                e = jnp.exp(-jnp.abs(v))
                soft = jnp.maximum(v, 0.0) + jnp.log(1.0 + e)
                sig = jnp.where(v >= 0.0, 1.0, e) / (1.0 + e)
                act[z, row + r] = (0.3 * v + 0.7 * soft).astype(act.dtype)
                g = (cot[z, row + r].astype(jnp.float32) * (0.3 + 0.7 * sig)).astype(gp.dtype)
                gp[z, row + r] = g
                gb[...] += g.astype(jnp.float32)
                line.append(g)
            grads.append(jnp.concatenate(line, axis=1))
        grad = jnp.concatenate(grads, axis=0)
        gk[...] += lax.dot_general(
            cells, grad, (((1,), (1,)), ((), ())), preferred_element_type=jnp.float32
        )


def backward_kernel(lo, mid, hi, w, out, taps):
    depth, rows, channels, columns = mid.shape
    ins = out.shape[2]
    clear_rim(taps)

    @pl.loop(0, rows)
    def _(row):
        fill(taps, 0, row, lo[row])
        for z in range(depth):
            fill(taps, z + 1, row, mid[z, row])
        fill(taps, depth + 1, row, hi[row])

    @pl.loop(0, rows // STEP)
    def _(step):
        row = step * STEP
        cells = patch(taps, row)
        res = jnp.dot(w[...], cells, preferred_element_type=jnp.float32)
        for z in range(depth):
            for r in range(STEP):
                out[z, row + r] = res[
                    z * ins : (z + 1) * ins, r * columns : (r + 1) * columns
                ].astype(out.dtype)


def banded(w, depth):
    outs, width = w.shape[1:]
    flat = w.transpose(1, 0, 2).reshape(outs, 3 * width)
    lines = [
        jnp.pad(flat, ((0, 0), (z * width, (depth - 1 - z) * width))) for z in range(depth)
    ]
    return jnp.concatenate(lines, axis=0)


def neighbours(planes):
    count = lax.axis_size("space")
    up = [(i, i + 1) for i in range(count - 1)]
    down = [(i + 1, i) for i in range(count - 1)]
    lo = lax.ppermute(planes[-1], "space", up)
    hi = lax.ppermute(planes[0], "space", down)
    return lo, hi


def local(volumes, kernel, bias, cotangent, finished_grads):
    volume = volumes[0].transpose(1, 2, 0, 3)
    cot = cotangent[0].transpose(1, 2, 0, 3)
    depth, rows, ins, columns = volume.shape
    outs = cot.shape[2]
    planes = depth + 2
    limit = pltpu.CompilerParams(vmem_limit_bytes=48 * 2**20)
    lo, hi = neighbours(volume)
    forward_w = banded(kernel.transpose(0, 3, 1, 2, 4).reshape(3, outs, 9 * ins), depth)
    backward_w = banded(
        kernel[::-1, ::-1, ::-1].transpose(0, 4, 1, 2, 3).reshape(3, ins, 9 * outs), depth
    )
    tall_bias = jnp.tile(bias, depth)[:, None]
    act, gp, gk, gb = pl.pallas_call(
        forward_kernel,
        out_shape=(
            jax.ShapeDtypeStruct((depth, rows, outs, columns), jnp.bfloat16),
            jax.ShapeDtypeStruct((depth, rows, outs, columns), jnp.bfloat16),
            jax.ShapeDtypeStruct((planes * 9 * ins, depth * outs), jnp.float32),
            jax.ShapeDtypeStruct((outs, columns), jnp.float32),
        ),
        in_specs=[VMEM] * 6,
        out_specs=(VMEM,) * 4,
        scratch_shapes=[pltpu.VMEM((planes, rows + 2, 3 * ins, columns), jnp.bfloat16)],
        compiler_params=limit,
        name="forward",
    )(lo, volume, hi, forward_w, tall_bias, cot)
    glo, ghi = neighbours(gp)
    gvol = pl.pallas_call(
        backward_kernel,
        out_shape=jax.ShapeDtypeStruct((depth, rows, ins, columns), jnp.bfloat16),
        in_specs=[VMEM] * 4,
        out_specs=VMEM,
        scratch_shapes=[pltpu.VMEM((planes, rows + 2, 3 * outs, columns), jnp.bfloat16)],
        compiler_params=limit,
        name="backward",
    )(glo, gp, ghi, backward_w)
    full = gk.reshape(planes, 3, 3, ins, depth, outs)
    taps = sum(full[z : z + 3, :, :, :, z] for z in range(depth)).transpose(0, 1, 2, 4, 3)
    bias_terms = jnp.sum(gb, axis=1)
    small = jnp.concatenate([taps.reshape(-1), bias_terms])
    summed = lax.psum(finished_grads.reshape(-1), ("dp", "space"))
    total = lax.psum(small, ("dp", "space"))
    count = lax.axis_size("dp") * lax.axis_size("space") * depth * rows * columns
    scale = 1.0 / math.sqrt(count)
    total = total * scale
    activations = act.transpose(2, 0, 1, 3)[None]
    grad_volumes = gvol.transpose(2, 0, 1, 3)[None]
    return (
        activations,
        grad_volumes,
        total[: taps.size].reshape(taps.shape),
        total[taps.size :],
        summed,
    )


def solution(mesh):
    slab = P("dp", None, "space", None, None)
    return jax.shard_map(
        local,
        mesh=mesh,
        in_specs=(slab, P(), P(), slab, P("dp", "space", None)),
        out_specs=(slab, slab, P(), P(), P()),
        check_vma=False,
    )
```

profile of v0, /device:TPU:0, one launch (start us, length us, event | category | flops | bytes accessed | tf_op | source)
XLA Modules:
  0.0 220.3 jit_solution(2806725018331667628)
XLA Ops:
  7.2 1.6 copy.32
  8.8 2.4 %collective-permute-start = (bf16[48,32,128]{2,1,0:T(8,128)(2,1)S(1)}, bf16[48,32,128]{2,1,0:T(8,128)(2,1)S(1)}, u32[]{:S(2)}, u32[]{:S(2)}) collective-permute-start(bf16[48,32,128]{2,1,0:T(8,128)(2,1)S(1)} %get-tuple-element.30), channel_id=1, source_target_pairs={{0,1},{1,2},{2,3},{3,4},{4,5},{5,6},{6,7},{8,9},{9,10},{10,11},{11... | collective-permute-start | bytes 1179656 | tf_op jit(solution)/shard_map/ppermute | solution.py:130
  11.3 1.4 collective-permute-start.1
  12.7 1.8 copy.31
  14.5 0.2 copy.17
  15.1 2.1 collective-permute-done.1.hi
  17.2 0.7 copy-done.2
  17.9 1.0 copy-done.3
  18.9 24.1 %forward.1 = (bf16[2,48,64,128]{3,2,1,0:T(8,128)(2,1)S(1)}, bf16[2,48,64,128]{3,2,1,0:T(8,128)(2,1)S(1)}, f32[1152,128]{1,0:T(8,128)S(1)}, f32[64,128]{1,0:T(8,128)S(1)}) custom-call(bf16[48,32,128]{2,1,0:T(8,128)(2,1)S(1)} %collective-permute-done.lo, bf16[2,48,32,128]{3,2,1,0:T(8,128)(2,1)S(1)} %bitcast.39, bf16[48,32,128]{2,1,0:T(8,128)(2,1)S(1)} %copy-done.3, ...), custom_call_target="tpu_custom_call" | custom-call | tf_op jit(solution)/shard_map/forward/pallas_call | solution.py:148
  43.1 1.1 copy-done
  44.2 0.7 reshape.40
  44.9 1.7 fusion.6
  46.6 1.6 copy.27
  48.3 1.5 copy.28
  49.8 2.2 add_bitcast_fusion
  52.0 1.4 reshape.41
  53.5 0.7 pad_maximum_fusion
  54.3 0.2 copy.20
  54.5 0.2 reshape.38
  55.0 1.3 slice_bitcast_fusion
  56.3 7.9 %collective-permute-start.2 = (bf16[48,64,128]{2,1,0:T(8,128)(2,1)}, bf16[48,64,128]{2,1,0:T(8,128)(2,1)S(1)}, u32[]{:S(2)}, u32[]{:S(2)}) collective-permute-start(bf16[48,64,128]{2,1,0:T(8,128)(2,1)} %get-tuple-element.26), channel_id=1, source_target_pairs={{0,1},{1,2},{2,3},{3,4},{4,5},{5,6},{6,7},{8,9},{9,10},{10,11},{11... | collective-permute-start | bytes 2359304 | tf_op jit(solution)/shard_map/ppermute | solution.py:130
  64.2 1.3 collective-permute-start.3
  65.5 2.2 copy.24
  67.7 124.6 %all-reduce.7.cloned.1.call-done = (f32[55360]{0:T(1024)}, f32[262144]{0:T(1024)}) async-done(((f32[55360]{0:T(1024)}, f32[262144]{0:T(1024)}), (f32[55360]{0:T(1024)}, f32[262144]{0:T(1024)})) %all-reduce.7.cloned.1.call-update) | async-done | bytes 1270032 | tf_op jit(solution)/shard_map/psum | solution.py:177
  192.3 1.0 broadcast_multiply_fusion
  193.3 0.7 slice.36
  194.0 0.5 slice.37
  194.5 1.2 reshape.42
  195.6 1.1 copy.26
  196.7 14.5 %backward.1 = bf16[2,48,32,128]{3,2,1,0:T(8,128)(2,1)S(1)} custom-call(bf16[48,64,128]{2,1,0:T(8,128)(2,1)S(1)} %collective-permute-done.2.lo, bf16[2,48,64,128]{3,2,1,0:T(8,128)(2,1)S(1)} %get-tuple-element.10.mid, bf16[48,64,128]{2,1,0:T(8,128)(2,1)} %collective-permute-done.3.hi, bf16[64,2304]{1,0:T(8,128)(2,1)S(1)} %fusion.4.w), custom_call_target="tpu_custom_call" | custom-call | tf_op jit(solution)/shard_map/backward/pallas_call | solution.py:163
  211.2 1.2 copy.25
  212.4 1.0 copy.36
  (30 shorter events, 1.0 us)
Async XLA Ops:
  7.2 185.1 %all-reduce.7.cloned.1.call-start = ((), (), s32[]{:S(2)}) async-start(), calls=%async_computation | async-start | bytes 2547712 | tf_op jit(solution)/shard_map/psum | solution.py:177
  7.2 5.5 %copy-start.4 = (bf16[1,64,2,48,128]{4,3,2,1,0:T(8,128)(2,1)S(1)}, bf16[1,64,2,48,128]{4,3,2,1,0:T(8,128)(2,1)}, u32[]{:S(2)}) copy-start(bf16[1,64,2,48,128]{4,3,2,1,0:T(8,128)(2,1)} %param.8) | copy-start | bytes 4718596
  8.8 6.2 %collective-permute-start = (bf16[48,32,128]{2,1,0:T(8,128)(2,1)S(1)}, bf16[48,32,128]{2,1,0:T(8,128)(2,1)S(1)}, u32[]{:S(2)}, u32[]{:S(2)}) collective-permute-start(bf16[48,32,128]{2,1,0:T(8,128)(2,1)S(1)} %get-tuple-element.30), channel_id=1, source_target_pairs={{0,1},{1,2},{2,3},{3,4},{4,5},{5,6},{6,7},{8,9},{9,10},{10,11},{11... | collective-permute-start | bytes 1179656 | tf_op jit(solution)/shard_map/ppermute | solution.py:130
  11.2 3.2 %copy-start.6 = (bf16[3,3,3,64,32]{3,4,2,1,0:T(8,128)(2,1)S(1)}, bf16[3,3,3,64,32]{3,4,2,1,0:T(8,128)(2,1)}, u32[]{:S(2)}) copy-start(bf16[3,3,3,64,32]{3,4,2,1,0:T(8,128)(2,1)} %param.6) | copy-start | bytes 331780
  11.2 3.6 %copy-start.8 = (f32[64]{0:T(128)S(1)}, f32[64]{0:T(128)}, u32[]{:S(2)}) copy-start(f32[64]{0:T(128)} %param.7) | copy-start | bytes 772
  11.3 5.9 %collective-permute-start.1 = (bf16[48,32,128]{2,1,0:T(8,128)(2,1)S(1)}, bf16[48,32,128]{2,1,0:T(8,128)(2,1)S(1)}, u32[]{:S(2)}, u32[]{:S(2)}) collective-permute-start(bf16[48,32,128]{2,1,0:T(8,128)(2,1)S(1)} %get-tuple-element.29), channel_id=1, source_target_pairs={{1,0},{2,1},{3,2},{4,3},{5,4},{6,5},{7,6},{9,8},{10,9},{11,10},{12... | collective-permute-start | bytes 1179656 | tf_op jit(solution)/shard_map/ppermute | solution.py:131
  17.2 0.7 copy-start.2
  17.9 1.0 copy-start.3
  43.0 1.1 copy-start
  52.0 2.3 %copy-start.7 = (bf16[3,3,3,64,32]{3,4,2,1,0:T(8,128)(2,1)S(1)}, bf16[3,3,3,64,32]{3,4,2,1,0:T(8,128)(2,1)}, u32[]{:S(2)}) copy-start(bf16[3,3,3,64,32]{3,4,2,1,0:T(8,128)(2,1)} %param.6) | copy-start | bytes 331780
  55.0 10.5 %copy-start.1 = (bf16[2,48,64,128]{3,2,1,0:T(8,128)(2,1)S(1)}, bf16[2,48,64,128]{3,2,1,0:T(8,128)(2,1)}, u32[]{:S(2)}) copy-start(bf16[2,48,64,128]{3,2,1,0:T(8,128)(2,1)} %copy-done) | copy-start | bytes 4718596
  56.3 140.4 %collective-permute-start.2 = (bf16[48,64,128]{2,1,0:T(8,128)(2,1)}, bf16[48,64,128]{2,1,0:T(8,128)(2,1)S(1)}, u32[]{:S(2)}, u32[]{:S(2)}) collective-permute-start(bf16[48,64,128]{2,1,0:T(8,128)(2,1)} %get-tuple-element.26), channel_id=1, source_target_pairs={{0,1},{1,2},{2,3},{3,4},{4,5},{5,6},{6,7},{8,9},{9,10},{10,11},{11... | collective-permute-start | bytes 2359304 | tf_op jit(solution)/shard_map/ppermute | solution.py:130
  64.2 132.5 %collective-permute-start.3 = (bf16[48,64,128]{2,1,0:T(8,128)(2,1)}, bf16[48,64,128]{2,1,0:T(8,128)(2,1)}, u32[]{:S(2)}, u32[]{:S(2)}) collective-permute-start(bf16[48,64,128]{2,1,0:T(8,128)(2,1)} %get-tuple-element.25), channel_id=1, source_target_pairs={{1,0},{2,1},{3,2},{4,3},{5,4},{6,5},{7,6},{9,8},{10,9},{11,10},{12... | collective-permute-start | bytes 2359304 | tf_op jit(solution)/shard_map/ppermute | solution.py:131
  211.2 1.2 copy-start.5
Sparse Core Ops, SparseCore 0:
  54.4 137.8 all-reduce.6
where the time goes:
time: 221 us; the launch traced here: 220 us
  waiting for transfers between devices  127 us (57%)
  Pallas kernels  38.6 us (17%)
  local copies, waits for them, and re-layouts  23.5 us (11%)
  between operations  14.3 us (6%)
  starting transfers between devices  13 us (6%)
  other arithmetic  4.16 us (2%)
    psum x1, waiting for transfers between devices, local(): total = lax.psum(small, ('dp', 'space'))  125 us
    pallas_call x1, Pallas kernels, local(): pl.pallas_call(forward_kernel, out_shape=(jax.ShapeDtypeStruct((depth, ro...  24.1 us
    unnamed x26, local copies, waits for them, and re-layouts  14.8 us
    pallas_call x1, Pallas kernels, local(): pl.pallas_call(backward_kernel, out_shape=jax.ShapeDtypeStruct((depth, ro...  14.5 us
    ppermute x2, starting transfers between devices, neighbours(): lo = lax.ppermute(planes[-1], 'space', up)  10.3 us
  transfers between devices with their start and end apart: 5, of which 2 were waited for; matrix products, arithmetic and copies ran while one was open for 5% of the time, Pallas kernels for 0%

commit v1 on v0

--- a/solution.py
+++ b/solution.py
@@ -10,6 +10,8 @@
 
 VMEM = pl.BlockSpec(memory_space=pltpu.VMEM)
 STEP = 2
+FORWARD_AT = ((1, 0), (2, 9), (3, 13), (4, 17))
+BACKWARD_AT = ((1, 0), (2, 5), (3, 10), (4, 15), (5, 20))
 
 
 def spread(block):
@@ -50,9 +52,120 @@
     return jnp.concatenate(tall, axis=0)
 
 
-def forward_kernel(lo, mid, hi, w, bias, cot, act, gp, gk, gb, taps):
+def ring_sizes():
+    return 2, lax.axis_size("dp"), lax.axis_size("space") // 2
+
+
+def copies_per_sum():
+    pair, line, deep = ring_sizes()
+    return 2 * (pair - 1 + line - 1 + deep - 1)
+
+
+def sum_scratch(rows, columns):
+    pair, line, deep = ring_sizes()
+    return [
+        pltpu.VMEM((line, deep, rows, columns), jnp.float32),
+        pltpu.VMEM((line - 1, deep, rows, columns), jnp.float32),
+        pltpu.VMEM((deep, rows, columns), jnp.float32),
+        pltpu.VMEM((deep - 1, rows, columns), jnp.float32),
+        pltpu.VMEM((pair, line, deep, rows, columns), jnp.float32),
+        pltpu.SemaphoreType.DMA((copies_per_sum(),)),
+        pltpu.SemaphoreType.DMA((copies_per_sum(),)),
+    ]
+
+
+class SumStages:
+    def __init__(self, x, total, half, from_line, quarter, from_deep, full, sends, recvs):
+        self.x, self.total, self.half, self.from_line = x, total, half, from_line
+        self.quarter, self.from_deep, self.full = quarter, from_deep, full
+        self.sends, self.recvs = sends, recvs
+        self.pair, self.line, self.deep = ring_sizes()
+        self.dp = lax.axis_index("dp")
+        space = lax.axis_index("space")
+        self.core, self.z = lax.rem(space, 2), space // 2
+        self.partners = [(self.dp, self.z * 2 + 1 - self.core)]
+        self.lines = [lax.rem(self.dp + t, self.line) for t in range(1, self.line)]
+        self.deeps = [lax.rem(self.z + t, self.deep) for t in range(1, self.deep)]
+        self.partners += [(p, space) for p in self.lines]
+        self.partners += [(self.dp, p * 2 + self.core) for p in self.deeps]
+
+    def greet(self):
+        barrier = pltpu.get_barrier_semaphore()
+        for other in self.partners:
+            pl.semaphore_signal(
+                barrier, inc=1, device_id=other, device_id_type=pl.DeviceIdType.MESH
+            )
+        pl.semaphore_wait(barrier, len(self.partners))
+
+    def copy(self, source, target, slot, other):
+        return pltpu.make_async_remote_copy(
+            src_ref=source,
+            dst_ref=target,
+            send_sem=self.sends.at[slot],
+            recv_sem=self.recvs.at[slot],
+            device_id=self.partners[other],
+            device_id_type=pl.DeviceIdType.MESH,
+        )
+
+    def moves(self, stage):
+        first_line, first_deep, second = 1, self.line, self.line + self.deep - 1
+        mine = self.full.at[self.core]
+        if stage == 0:
+            return [self.copy(self.x.at[1 - self.core], self.half, 0, 0)]
+        if stage == 1:
+            return [
+                self.copy(self.half.at[p], self.from_line.at[t], first_line + t, first_line + t)
+                for t, p in enumerate(self.lines)
+            ]
+        if stage == 2:
+            return [
+                self.copy(self.quarter.at[p], self.from_deep.at[t], first_deep + t, first_deep + t)
+                for t, p in enumerate(self.deeps)
+            ]
+        if stage == 3:
+            own = mine.at[self.dp, self.z]
+            return [
+                self.copy(own, own, second + first_deep + t, first_deep + t)
+                for t in range(len(self.deeps))
+            ]
+        if stage == 4:
+            own = mine.at[self.dp]
+            return [
+                self.copy(own, own, second + first_line + t, first_line + t)
+                for t in range(len(self.lines))
+            ]
+        return [self.copy(mine, mine, second, 0)]
+
+    def run(self, stage):
+        if stage > 0:
+            for move in self.moves(stage - 1):
+                move.wait()
+        if stage == 1:
+            self.half[...] += self.x[self.core]
+        if stage == 2:
+            value = self.half[self.dp]
+            for t in range(len(self.lines)):
+                value += self.from_line[t]
+            self.quarter[...] = value
+        if stage == 3:
+            value = self.quarter[self.z]
+            for t in range(len(self.deeps)):
+                value += self.from_deep[t]
+            self.full[self.core, self.dp, self.z] = value
+        if stage < 6:
+            for move in self.moves(stage):
+                move.start()
+        else:
+            self.total[...] = self.full[...]
+
+
+def forward_kernel(lo, mid, hi, w, bias, cot, x, act, gp, small, total, taps, gk, *scratch):
     depth, rows, channels, columns = mid.shape
     outs = cot.shape[2]
+    plane = 9 * channels
+    stages = SumStages(x, total, *scratch)
+    stages.greet()
+    stages.run(0)
     clear_rim(taps)
 
     @pl.loop(0, rows)
@@ -63,10 +176,16 @@
         fill(taps, depth + 1, row, hi[row])
 
     gk[...] = jnp.zeros_like(gk)
-    gb[...] = jnp.zeros_like(gb)
-
-    @pl.loop(0, rows // STEP)
+    steps = rows // STEP
+
+    @pl.loop(0, steps)
     def _(step):
+        for stage, at in FORWARD_AT:
+
+            @pl.when(step == steps * at // 24)
+            def _():
+                stages.run(stage)
+
         row = step * STEP
         cells = patch(taps, row)
         pre = jnp.dot(w[...], cells, preferred_element_type=jnp.float32) + bias[...]
@@ -81,18 +200,37 @@
                 act[z, row + r] = (0.3 * v + 0.7 * soft).astype(act.dtype)
                 g = (cot[z, row + r].astype(jnp.float32) * (0.3 + 0.7 * sig)).astype(gp.dtype)
                 gp[z, row + r] = g
-                gb[...] += g.astype(jnp.float32)
                 line.append(g)
             grads.append(jnp.concatenate(line, axis=1))
         grad = jnp.concatenate(grads, axis=0)
+        ones = jnp.ones((16, STEP * columns), cells.dtype)
         gk[...] += lax.dot_general(
-            cells, grad, (((1,), (1,)), ((), ())), preferred_element_type=jnp.float32
+            jnp.concatenate([cells, ones], axis=0),
+            grad,
+            (((1,), (1,)), ((), ())),
+            preferred_element_type=jnp.float32,
         )
 
-
-def backward_kernel(lo, mid, hi, w, out, taps):
+    small[...] = jnp.zeros_like(small)
+    tall = 3 * plane
+    ends = (depth + 2) * plane
+    value = gk[0:tall, 0:outs]
+    extra = gk[ends : ends + 8, 0:outs]
+    for z in range(1, depth):
+        value += gk[z * plane : z * plane + tall, z * outs : (z + 1) * outs]
+        extra += gk[ends : ends + 8, z * outs : (z + 1) * outs]
+    small[0 : tall // 2, :] = jnp.concatenate([value[: tall // 2], value[tall // 2 :]], axis=1)
+    small[tall // 2 : tall // 2 + 8, :] = jnp.concatenate([extra, extra], axis=1)
+    stages.run(5)
+    stages.run(6)
+
+
+def backward_kernel(lo, mid, hi, w, x, out, total, taps, *scratch):
     depth, rows, channels, columns = mid.shape
     ins = out.shape[2]
+    stages = SumStages(x, total, *scratch)
+    stages.greet()
+    stages.run(0)
     clear_rim(taps)
 
     @pl.loop(0, rows)
@@ -102,8 +240,16 @@
             fill(taps, z + 1, row, mid[z, row])
         fill(taps, depth + 1, row, hi[row])
 
-    @pl.loop(0, rows // STEP)
+    steps = rows // STEP
+
+    @pl.loop(0, steps)
     def _(step):
+        for stage, at in BACKWARD_AT:
+
+            @pl.when(step == steps * at // 24)
+            def _():
+                stages.run(stage)
+
         row = step * STEP
         cells = patch(taps, row)
         res = jnp.dot(w[...], cells, preferred_element_type=jnp.float32)
@@ -113,6 +259,8 @@
                     z * ins : (z + 1) * ins, r * columns : (r + 1) * columns
                 ].astype(out.dtype)
 
+    stages.run(6)
+
 
 def banded(w, depth):
     outs, width = w.shape[1:]
@@ -138,54 +286,74 @@
     depth, rows, ins, columns = volume.shape
     outs = cot.shape[2]
     planes = depth + 2
-    limit = pltpu.CompilerParams(vmem_limit_bytes=48 * 2**20)
     lo, hi = neighbours(volume)
     forward_w = banded(kernel.transpose(0, 3, 1, 2, 4).reshape(3, outs, 9 * ins), depth)
     backward_w = banded(
         kernel[::-1, ::-1, ::-1].transpose(0, 4, 1, 2, 3).reshape(3, ins, 9 * outs), depth
     )
     tall_bias = jnp.tile(bias, depth)[:, None]
-    act, gp, gk, gb = pl.pallas_call(
+    sizes = ring_sizes()
+    devices = math.prod(sizes)
+
+    def share(count):
+        return 8 * math.ceil(count / (columns * devices * 8))
+
+    entries = finished_grads.size
+    parts = share(entries)
+    flat = jnp.pad(finished_grads.reshape(-1), (0, parts * columns * devices - entries))
+    tall = 27 * ins // 2
+    small_parts = share((tall + 8) * columns)
+    act, gp, small, summed = pl.pallas_call(
         forward_kernel,
         out_shape=(
             jax.ShapeDtypeStruct((depth, rows, outs, columns), jnp.bfloat16),
             jax.ShapeDtypeStruct((depth, rows, outs, columns), jnp.bfloat16),
-            jax.ShapeDtypeStruct((planes * 9 * ins, depth * outs), jnp.float32),
-            jax.ShapeDtypeStruct((outs, columns), jnp.float32),
+            jax.ShapeDtypeStruct((small_parts * devices, columns), jnp.float32),
+            jax.ShapeDtypeStruct((*sizes, parts, columns), jnp.float32),
         ),
-        in_specs=[VMEM] * 6,
+        in_specs=[VMEM] * 7,
         out_specs=(VMEM,) * 4,
-        scratch_shapes=[pltpu.VMEM((planes, rows + 2, 3 * ins, columns), jnp.bfloat16)],
-        compiler_params=limit,
+        scratch_shapes=[
+            pltpu.VMEM((planes, rows + 2, 3 * ins, columns), jnp.bfloat16),
+            pltpu.VMEM((planes * 9 * ins + 16, depth * outs), jnp.float32),
+            *sum_scratch(parts, columns),
+        ],
+        compiler_params=pltpu.CompilerParams(
+            vmem_limit_bytes=48 * 2**20, collective_id=0, has_side_effects=True
+        ),
         name="forward",
-    )(lo, volume, hi, forward_w, tall_bias, cot)
+    )(lo, volume, hi, forward_w, tall_bias, cot, flat.reshape(*sizes, parts, columns))
     glo, ghi = neighbours(gp)
-    gvol = pl.pallas_call(
+    gvol, small_sum = pl.pallas_call(
         backward_kernel,
-        out_shape=jax.ShapeDtypeStruct((depth, rows, ins, columns), jnp.bfloat16),
-        in_specs=[VMEM] * 4,
-        out_specs=VMEM,
-        scratch_shapes=[pltpu.VMEM((planes, rows + 2, 3 * outs, columns), jnp.bfloat16)],
-        compiler_params=limit,
+        out_shape=(
+            jax.ShapeDtypeStruct((depth, rows, ins, columns), jnp.bfloat16),
+            jax.ShapeDtypeStruct((*sizes, small_parts, columns), jnp.float32),
+        ),
+        in_specs=[VMEM] * 5,
+        out_specs=(VMEM,) * 2,
+        scratch_shapes=[
+            pltpu.VMEM((planes, rows + 2, 3 * outs, columns), jnp.bfloat16),
+            *sum_scratch(small_parts, columns),
+        ],
+        compiler_params=pltpu.CompilerParams(
+            vmem_limit_bytes=48 * 2**20, collective_id=1, has_side_effects=True
+        ),
         name="backward",
-    )(glo, gp, ghi, backward_w)
-    full = gk.reshape(planes, 3, 3, ins, depth, outs)
-    taps = sum(full[z : z + 3, :, :, :, z] for z in range(depth)).transpose(0, 1, 2, 4, 3)
-    bias_terms = jnp.sum(gb, axis=1)
-    small = jnp.concatenate([taps.reshape(-1), bias_terms])
-    summed = lax.psum(finished_grads.reshape(-1), ("dp", "space"))
-    total = lax.psum(small, ("dp", "space"))
+    )(glo, gp, ghi, backward_w, small.reshape(*sizes, small_parts, columns))
     count = lax.axis_size("dp") * lax.axis_size("space") * depth * rows * columns
     scale = 1.0 / math.sqrt(count)
-    total = total * scale
+    lines = small_sum.reshape(-1, columns)
+    halves = [lines[:tall, h * outs : (h + 1) * outs] for h in range(2)]
+    taps = jnp.concatenate(halves, axis=0).reshape(3, 3, 3, ins, outs)
     activations = act.transpose(2, 0, 1, 3)[None]
     grad_volumes = gvol.transpose(2, 0, 1, 3)[None]
     return (
         activations,
         grad_volumes,
-        total[: taps.size].reshape(taps.shape),
-        total[taps.size :],
-        summed,
+        taps.transpose(0, 1, 2, 4, 3) * scale,
+        lines[tall, :outs] * scale,
+        summed.reshape(-1)[:entries],
     )
 
 

time: 221 us -> 103 us (0.47)
  waiting for transfers between devices: 127 us -> 1.55 us
  Pallas kernels: 38.6 us -> 72.8 us
  between operations: 14.3 us -> 0.89 us
  starting transfers between devices: 13 us -> 7.4 us
  local copies, waits for them, and re-layouts: 23.5 us -> 18 us
  other arithmetic: 4.16 us -> 1.53 us
    psum x1 -> x0, waiting for transfers between devices: 125 us -> none  [local(): total = lax.psum(small, ('dp', 'space'))]
    pallas_call x1, Pallas kernels: 14.5 us -> 32.8 us  [local(): pl.pallas_call(backward_kernel, out_shape=(jax.ShapeDtypeStruct((depth, r...]
    pallas_call x1, Pallas kernels: 24.1 us -> 40 us  [local(): pl.pallas_call(forward_kernel, out_shape=(jax.ShapeDtypeStruct((depth, ro...]
    ppermute x2, starting transfers between devices: 10.3 us -> 4.68 us  [neighbours(): lo = lax.ppermute(planes[-1], 'space', up)]
    unnamed x26 -> x33, local copies, waits for them, and re-layouts: 14.8 us -> 11.2 us
    reshape x3 -> x0, local copies, waits for them, and re-layouts: 3.28 us -> none  [the longest x1 1.44 us: local(): small = jnp.concatenate([taps.reshape(-1), bias_terms])]
    slice x3 -> x1, local copies, waits for them, and re-layouts: 2.95 us -> 0.12 us  [local(): halves = [lines[:tall, h * outs:(h + 1) * outs] for h in range(2)]]
    squeeze x2, local copies, waits for them, and re-layouts: 1.31 us -> 4.06 us  [neighbours(): hi = lax.ppermute(planes[0], 'space', down)]
  transfers between devices with their start and end apart: 5 -> 4, of which waited for: 2 -> 1; matrix products, arithmetic and copies ran while one was open for 5% -> 7% of each run, Pallas kernels for 0% -> 0%
where the time goes in v1:
time: 103 us; the launch traced here: 102 us
  Pallas kernels  72.8 us (71%)
  local copies, waits for them, and re-layouts  18 us (17%)
  starting transfers between devices  7.4 us (7%)
  waiting for transfers between devices  1.55 us (2%)
  other arithmetic  1.53 us (1%)
    pallas_call x1, Pallas kernels, local(): pl.pallas_call(forward_kernel, out_shape=(jax.ShapeDtypeStruct((depth, ro...  40 us
    pallas_call x1, Pallas kernels, local(): pl.pallas_call(backward_kernel, out_shape=(jax.ShapeDtypeStruct((depth, r...  32.8 us
    unnamed x33, local copies, waits for them, and re-layouts  11.2 us
    ppermute x2, starting transfers between devices, neighbours(): lo = lax.ppermute(planes[-1], 'space', up)  4.68 us
    squeeze x2, local copies, waits for them, and re-layouts, neighbours(): hi = lax.ppermute(planes[0], 'space', down)  4.06 us
    ppermute x2, starting transfers between devices, neighbours(): hi = lax.ppermute(planes[0], 'space', down)  2.72 us
  transfers between devices with their start and end apart: 4, of which 1 were waited for; matrix products, arithmetic and copies ran while one was open for 7% of the time, Pallas kernels for 0%

profile of v1, /device:TPU:0, one launch (start us, length us, event | category | flops | bytes accessed | tf_op | source)
XLA Modules:
  0.0 102.2 jit_solution(12566020753205240176)
XLA Ops:
  0.6 1.6 %copy.27 = bf16[1,32,2,48,128]{4,1,3,2,0:T(8,128)(2,1)S(1)} copy(bf16[1,32,2,48,128]{4,3,2,1,0:T(8,128)(2,1)} %param.5) | data formatting | bytes 1572864 | tf_op args[0]
  2.2 0.9 slice_bitcast_fusion.2
  3.1 2.4 %collective-permute-start = (bf16[48,32,128]{2,1,0:T(8,128)(2,1)}, bf16[48,32,128]{2,1,0:T(8,128)(2,1)S(1)}, u32[]{:S(2)}, u32[]{:S(2)}) collective-permute-start(bf16[48,32,128]{2,1,0:T(8,128)(2,1)} %get-tuple-element.30), channel_id=1, source_target_pairs={{0,1},{1,2},{2,3},{3,4},{4,5},{5,6},{6,7},{8,9},{9,10},{10,11},{11... | collective-permute-start | bytes 1179656 | tf_op jit(solution)/shard_map/ppermute | solution.py:278
  5.5 0.0 copy-start.11
  5.5 0.0 copy-start.13
  5.5 1.4 %collective-permute-start.1 = (bf16[48,32,128]{2,1,0:T(8,128)(2,1)}, bf16[48,32,128]{2,1,0:T(8,128)(2,1)S(1)}, u32[]{:S(2)}, u32[]{:S(2)}) collective-permute-start(bf16[48,32,128]{2,1,0:T(8,128)(2,1)} %get-tuple-element.29), channel_id=1, source_target_pairs={{1,0},{2,1},{3,2},{4,3},{5,4},{6,5},{7,6},{9,8},{10,9},{11,10},{12... | collective-permute-start | bytes 1179656 | tf_op jit(solution)/shard_map/ppermute | solution.py:279
  7.0 1.8 %copy.26 = bf16[1,64,2,48,128]{4,1,3,2,0:T(8,128)(2,1)} copy(bf16[1,64,2,48,128]{4,3,2,1,0:T(8,128)(2,1)S(1)} %copy-done.10) | data formatting | bytes 3145728 | tf_op args[3]
  8.7 0.2 copy.17
  8.9 0.1 reshape.43
  9.1 0.1 broadcast_in_dim_tile.4.bias
  9.3 0.1 fusion.5.w
  9.4 0.7 copy-done.4
  10.1 1.5 %collective-permute-done.1.hi = bf16[48,32,128]{2,1,0:T(8,128)(2,1)S(1)} collective-permute-done((bf16[48,32,128]{2,1,0:T(8,128)(2,1)}, bf16[48,32,128]{2,1,0:T(8,128)(2,1)S(1)}, u32[]{:S(2)}, u32[]{:S(2)}) %collective-permute-start.1) | collective-permute-done | bytes 393248 | tf_op jit(solution)/shard_map/ppermute | solution.py:279
  11.7 0.7 copy-done.6
  12.4 1.0 copy-done.5
  13.4 1.0 copy-done.7
  14.4 40.0 %forward.1 = (bf16[2,48,64,128]{3,2,1,0:T(8,128)(2,1)S(1)}, bf16[2,48,64,128]{3,2,1,0:T(8,128)(2,1)}, f32[512,128]{1,0:T(8,128)S(1)}, f32[2,4,4,64,128]{4,3,2,1,0:T(8,128)S(1)}) custom-call(bf16[48,32,128]{2,1,0:T(8,128)(2,1)S(1)} %copy-done.5, bf16[2,48,32,128]{3,2,1,0:T(8,128)(2,1)S(1)} %bitcast.41, bf16[48,32,128]{2,1,0:T(8,128)(2,1)S(1)} %copy-done.7, ...), custom_call_target="tpu_custom_call" | custom-call | tf_op jit(solution)/shard_map/forward/pallas_call | solution.py:306
  54.5 3.1 %slice_bitcast_fusion = (bf16[48,64,128]{2,1,0:T(8,128)(2,1)}, bf16[48,64,128]{2,1,0:T(8,128)(2,1)}) fusion(bf16[2,48,64,128]{3,2,1,0:T(8,128)(2,1)} %get-tuple-element.12.mid), kind=kLoop, calls=%fused_computation.2 | loop fusion | bytes 3145728 | tf_op jit(solution)/shard_map/squeeze | solution.py:279
  57.6 2.3 %collective-permute-start.2 = (bf16[48,64,128]{2,1,0:T(8,128)(2,1)}, bf16[48,64,128]{2,1,0:T(8,128)(2,1)S(1)}, u32[]{:S(2)}, u32[]{:S(2)}) collective-permute-start(bf16[48,64,128]{2,1,0:T(8,128)(2,1)} %get-tuple-element.28), channel_id=1, source_target_pairs={{0,1},{1,2},{2,3},{3,4},{4,5},{5,6},{6,7},{8,9},{9,10},{10,11},{11... | collective-permute-start | bytes 2359304 | tf_op jit(solution)/shard_map/ppermute | solution.py:278
  60.0 1.3 %collective-permute-start.3 = (bf16[48,64,128]{2,1,0:T(8,128)(2,1)}, bf16[48,64,128]{2,1,0:T(8,128)(2,1)S(1)}, u32[]{:S(2)}, u32[]{:S(2)}) collective-permute-start(bf16[48,64,128]{2,1,0:T(8,128)(2,1)} %get-tuple-element.27), channel_id=1, source_target_pairs={{1,0},{2,1},{3,2},{4,3},{5,4},{6,5},{7,6},{9,8},{10,9},{11,10},{12... | collective-permute-start | bytes 2359304 | tf_op jit(solution)/shard_map/ppermute | solution.py:279
  61.3 0.2 copy.20
  61.5 0.9 reshape.45
  62.3 1.0 copy.21
  63.3 0.1 reshape.46
  63.4 0.1 fusion.4.w
  63.6 2.2 %copy.22 = bf16[1,64,2,48,128]{4,3,2,1,0:T(8,128)(2,1)} copy(bf16[1,64,2,48,128]{4,1,3,2,0:T(8,128)(2,1)S(1)} %bitcast.42) | data formatting | bytes 3145728
  65.8 32.8 %backward.1 = (bf16[2,48,32,128]{3,2,1,0:T(8,128)(2,1)S(1)}, f32[2,4,4,16,128]{4,3,2,1,0:T(8,128)S(1)}) custom-call(bf16[48,64,128]{2,1,0:T(8,128)(2,1)S(1)} %collective-permute-done.2.lo, bf16[2,48,64,128]{3,2,1,0:T(8,128)(2,1)S(1)} %copy-done, bf16[48,64,128]{2,1,0:T(8,128)(2,1)S(1)} %collective-permute-done.3.hi, bf16[64,2304]{1,0:T(8,128)(2,1)S(1)} %fusion.4.w, ...), custom_call_target="tpu_custom_call" | custom-call | tf_op jit(solution)/shard_map/backward/pallas_call | solution.py:327
  98.6 0.1 fusion.7
  98.7 0.5 fusion.6
  99.2 1.2 %copy.23 = bf16[1,32,2,48,128]{4,3,2,1,0:T(8,128)(2,1)} copy(bf16[1,32,2,48,128]{4,1,3,2,0:T(8,128)(2,1)S(1)} %bitcast.45) | data formatting | bytes 1572864
  100.4 0.8 maximum_multiply_fusion
  101.2 1.0 %copy.29 = f32[262144]{0:T(1024)} copy(f32[262144]{0:T(1024)S(1)} %bitcast.44) | data formatting | bytes 2097152
  (27 shorter events, 0.1 us)
Async XLA Ops:
  0.6 6.3 %copy-start.10 = (bf16[1,64,2,48,128]{4,3,2,1,0:T(8,128)(2,1)S(1)}, bf16[1,64,2,48,128]{4,3,2,1,0:T(8,128)(2,1)}, u32[]{:S(2)}) copy-start(bf16[1,64,2,48,128]{4,3,2,1,0:T(8,128)(2,1)} %param.8) | copy-start | bytes 4718596
  3.1 6.2 %collective-permute-start = (bf16[48,32,128]{2,1,0:T(8,128)(2,1)}, bf16[48,32,128]{2,1,0:T(8,128)(2,1)S(1)}, u32[]{:S(2)}, u32[]{:S(2)}) collective-permute-start(bf16[48,32,128]{2,1,0:T(8,128)(2,1)} %get-tuple-element.30), channel_id=1, source_target_pairs={{0,1},{1,2},{2,3},{3,4},{4,5},{5,6},{6,7},{8,9},{9,10},{10,11},{11... | collective-permute-start | bytes 1179656 | tf_op jit(solution)/shard_map/ppermute | solution.py:278
  5.5 3.2 %copy-start.11 = (bf16[3,3,3,64,32]{3,4,2,1,0:T(8,128)(2,1)S(1)}, bf16[3,3,3,64,32]{3,4,2,1,0:T(8,128)(2,1)}, u32[]{:S(2)}) copy-start(bf16[3,3,3,64,32]{3,4,2,1,0:T(8,128)(2,1)} %param.6) | copy-start | bytes 331780
  5.5 3.6 %copy-start.13 = (f32[64]{0:T(128)S(1)}, f32[64]{0:T(128)}, u32[]{:S(2)}) copy-start(f32[64]{0:T(128)} %param.7) | copy-start | bytes 772
  5.5 6.9 %copy-start.1 = (f32[1,1,262144]{2,1,0:T(1,128)S(1)}, f32[1,1,262144]{2,1,0:T(1,128)}, u32[]{:S(2)}) copy-start(f32[1,1,262144]{2,1,0:T(1,128)} %param.9) | copy-start | bytes 3145732
  5.5 6.1 %collective-permute-start.1 = (bf16[48,32,128]{2,1,0:T(8,128)(2,1)}, bf16[48,32,128]{2,1,0:T(8,128)(2,1)S(1)}, u32[]{:S(2)}, u32[]{:S(2)}) collective-permute-start(bf16[48,32,128]{2,1,0:T(8,128)(2,1)} %get-tuple-element.29), channel_id=1, source_target_pairs={{1,0},{2,1},{3,2},{4,3},{5,4},{6,5},{7,6},{9,8},{10,9},{11,10},{12... | collective-permute-start | bytes 1179656 | tf_op jit(solution)/shard_map/ppermute | solution.py:279
  9.4 0.7 copy-start.4
  11.7 0.7 copy-start.6
  12.4 1.0 copy-start.5
  13.4 1.0 copy-start.7
  54.5 3.2 %copy-start.2 = (f32[2,4,4,64,128]{4,3,2,1,0:T(8,128)}, f32[2,4,4,64,128]{4,3,2,1,0:T(8,128)S(1)}, u32[]{:S(2)}) copy-start(f32[2,4,4,64,128]{4,3,2,1,0:T(8,128)S(1)} %get-tuple-element.16) | copy-start | bytes 3145732
  54.5 3.2 %copy-start.8 = (f32[512,128]{1,0:T(8,128)}, f32[512,128]{1,0:T(8,128)S(1)}, u32[]{:S(2)}) copy-start(f32[512,128]{1,0:T(8,128)S(1)} %get-tuple-element.13) | copy-start | bytes 786436
  54.5 6.8 %copy-start.12 = (bf16[3,3,3,64,32]{3,4,2,1,0:T(8,128)(2,1)S(1)}, bf16[3,3,3,64,32]{3,4,2,1,0:T(8,128)(2,1)}, u32[]{:S(2)}) copy-start(bf16[3,3,3,64,32]{3,4,2,1,0:T(8,128)(2,1)} %param.6) | copy-start | bytes 331780
  57.6 8.1 %collective-permute-start.2 = (bf16[48,64,128]{2,1,0:T(8,128)(2,1)}, bf16[48,64,128]{2,1,0:T(8,128)(2,1)S(1)}, u32[]{:S(2)}, u32[]{:S(2)}) collective-permute-start(bf16[48,64,128]{2,1,0:T(8,128)(2,1)} %get-tuple-element.28), channel_id=1, source_target_pairs={{0,1},{1,2},{2,3},{3,4},{4,5},{5,6},{6,7},{8,9},{9,10},{10,11},{11... | collective-permute-start | bytes 2359304 | tf_op jit(solution)/shard_map/ppermute | solution.py:278
  60.0 5.8 %collective-permute-start.3 = (bf16[48,64,128]{2,1,0:T(8,128)(2,1)}, bf16[48,64,128]{2,1,0:T(8,128)(2,1)S(1)}, u32[]{:S(2)}, u32[]{:S(2)}) collective-permute-start(bf16[48,64,128]{2,1,0:T(8,128)(2,1)} %get-tuple-element.27), channel_id=1, source_target_pairs={{1,0},{2,1},{3,2},{4,3},{5,4},{6,5},{7,6},{9,8},{10,9},{11,10},{12... | collective-permute-start | bytes 2359304 | tf_op jit(solution)/shard_map/ppermute | solution.py:279
  63.6 2.2 %copy-start = (bf16[2,48,64,128]{3,2,1,0:T(8,128)(2,1)S(1)}, bf16[2,48,64,128]{3,2,1,0:T(8,128)(2,1)}, u32[]{:S(2)}) copy-start(bf16[2,48,64,128]{3,2,1,0:T(8,128)(2,1)} %get-tuple-element.12.mid) | copy-start | bytes 4718596
  63.6 2.2 %copy-start.9 = (f32[512,128]{1,0:T(8,128)S(1)}, f32[512,128]{1,0:T(8,128)}, u32[]{:S(2)}) copy-start(f32[512,128]{1,0:T(8,128)} %copy-done.8) | copy-start | bytes 786436
  98.6 2.7 %copy-start.3 = (f32[2,4,4,64,128]{4,3,2,1,0:T(8,128)S(1)}, f32[2,4,4,64,128]{4,3,2,1,0:T(8,128)}, u32[]{:S(2)}) copy-start(f32[2,4,4,64,128]{4,3,2,1,0:T(8,128)} %copy-done.2) | copy-start | bytes 3145732

commit v2 on v1

--- a/solution.py
+++ b/solution.py
@@ -10,7 +10,9 @@
 
 VMEM = pl.BlockSpec(memory_space=pltpu.VMEM)
 STEP = 2
-FORWARD_AT = ((1, 0), (2, 9), (3, 13), (4, 17))
+PARTS = 4
+FORWARD_AT = ((1, 1), (2, 11), (3, 16), (4, 20))
+WIDE_AT = ((5, 6),)
 BACKWARD_AT = ((1, 0), (2, 5), (3, 10), (4, 15), (5, 20))
 
 
@@ -89,13 +91,14 @@
         self.partners += [(p, space) for p in self.lines]
         self.partners += [(self.dp, p * 2 + self.core) for p in self.deeps]
 
-    def greet(self):
+    def greet(self, *more):
         barrier = pltpu.get_barrier_semaphore()
-        for other in self.partners:
+        others = [*self.partners, *more]
+        for other in others:
             pl.semaphore_signal(
                 barrier, inc=1, device_id=other, device_id_type=pl.DeviceIdType.MESH
             )
-        pl.semaphore_wait(barrier, len(self.partners))
+        pl.semaphore_wait(barrier, len(others))
 
     def copy(self, source, target, slot, other):
         return pltpu.make_async_remote_copy(
@@ -159,24 +162,90 @@
             self.total[...] = self.full[...]
 
 
-def forward_kernel(lo, mid, hi, w, bias, cot, x, act, gp, small, total, taps, gk, *scratch):
+def fused_kernel(
+    mid, w, back_w, bias, cot, x, act, out, small_total, total,
+    taps, back_taps, gk, gp, lo, hi, glo, ghi, small,
+    halo_sends, halo_recvs, grad_sends, grad_recvs, *scratch
+):
     depth, rows, channels, columns = mid.shape
     outs = cot.shape[2]
     plane = 9 * channels
-    stages = SumStages(x, total, *scratch)
-    stages.greet()
-    stages.run(0)
+    steps = rows // STEP
+    part = rows // PARTS
+    space = lax.axis_index("space")
+    dp = lax.axis_index("dp")
+    last = lax.axis_size("space") - 1
+    half = len(scratch) // 2
+    wide = SumStages(x, total, *scratch[:half])
+    late = SumStages(small, small_total, *scratch[half:])
+    other = lax.rem(space + 2 * lax.rem(space, 2) + last, last + 1)
+    wide.greet((dp, other))
+
+    def push(source, target, send, recv, to):
+        return pltpu.make_async_remote_copy(
+            src_ref=source,
+            dst_ref=target,
+            send_sem=send,
+            recv_sem=recv,
+            device_id=(dp, to),
+            device_id_type=pl.DeviceIdType.MESH,
+        )
+
+    def volume_down():
+        return push(mid.at[0], hi, halo_sends.at[0], halo_recvs.at[0], space - 1)
+
+    def volume_up():
+        return push(mid.at[depth - 1], lo, halo_sends.at[1], halo_recvs.at[1], space + 1)
+
+    def grad_down(n):
+        at = pl.ds(n * part, part)
+        return push(gp.at[0, at], ghi.at[at], grad_sends.at[0, n], grad_recvs.at[0, n], space - 1)
+
+    def grad_up(n):
+        at = pl.ds(n * part, part)
+        return push(
+            gp.at[depth - 1, at], glo.at[at], grad_sends.at[1, n], grad_recvs.at[1, n], space + 1
+        )
+
+    @pl.when(space > 0)
+    def _():
+        volume_down().start()
+
+    @pl.when(space < last)
+    def _():
+        volume_up().start()
+
+    wide.run(0)
     clear_rim(taps)
+    clear_rim(back_taps)
 
     @pl.loop(0, rows)
     def _(row):
-        fill(taps, 0, row, lo[row])
         for z in range(depth):
             fill(taps, z + 1, row, mid[z, row])
-        fill(taps, depth + 1, row, hi[row])
-
+
+    def rim(target, plane_in, edge):
+        @pl.when(space == (last if edge else 0))
+        def _():
+            plane_in[...] = jnp.zeros_like(plane_in)
+
+        @pl.loop(0, rows)
+        def _(row):
+            fill(target, depth + 1 if edge else 0, row, plane_in[row])
+
+    @pl.when(space > 0)
+    def _():
+        volume_down().wait_send()
+        volume_up().wait_recv()
+
+    @pl.when(space < last)
+    def _():
+        volume_up().wait_send()
+        volume_down().wait_recv()
+
+    rim(taps, lo, 0)
+    rim(taps, hi, 1)
     gk[...] = jnp.zeros_like(gk)
-    steps = rows // STEP
 
     @pl.loop(0, steps)
     def _(step):
@@ -184,7 +253,7 @@
 
             @pl.when(step == steps * at // 24)
             def _():
-                stages.run(stage)
+                wide.run(stage)
 
         row = step * STEP
         cells = patch(taps, row)
@@ -200,6 +269,7 @@
                 act[z, row + r] = (0.3 * v + 0.7 * soft).astype(act.dtype)
                 g = (cot[z, row + r].astype(jnp.float32) * (0.3 + 0.7 * sig)).astype(gp.dtype)
                 gp[z, row + r] = g
+                fill(back_taps, z + 1, row + r, g)
                 line.append(g)
             grads.append(jnp.concatenate(line, axis=1))
         grad = jnp.concatenate(grads, axis=0)
@@ -210,8 +280,18 @@
             (((1,), (1,)), ((), ())),
             preferred_element_type=jnp.float32,
         )
-
-    small[...] = jnp.zeros_like(small)
+        for n in range(PARTS):
+
+            @pl.when(step == (n + 1) * steps // PARTS - 1)
+            def _():
+                @pl.when(space > 0)
+                def _():
+                    grad_down(n).start()
+
+                @pl.when(space < last)
+                def _():
+                    grad_up(n).start()
+
     tall = 3 * plane
     ends = (depth + 2) * plane
     value = gk[0:tall, 0:outs]
@@ -219,47 +299,56 @@
     for z in range(1, depth):
         value += gk[z * plane : z * plane + tall, z * outs : (z + 1) * outs]
         extra += gk[ends : ends + 8, z * outs : (z + 1) * outs]
-    small[0 : tall // 2, :] = jnp.concatenate([value[: tall // 2], value[tall // 2 :]], axis=1)
-    small[tall // 2 : tall // 2 + 8, :] = jnp.concatenate([extra, extra], axis=1)
-    stages.run(5)
-    stages.run(6)
-
-
-def backward_kernel(lo, mid, hi, w, x, out, total, taps, *scratch):
-    depth, rows, channels, columns = mid.shape
-    ins = out.shape[2]
-    stages = SumStages(x, total, *scratch)
-    stages.greet()
-    stages.run(0)
-    clear_rim(taps)
-
-    @pl.loop(0, rows)
-    def _(row):
-        fill(taps, 0, row, lo[row])
-        for z in range(depth):
-            fill(taps, z + 1, row, mid[z, row])
-        fill(taps, depth + 1, row, hi[row])
-
-    steps = rows // STEP
+    lines = small.size // columns
+    small[...] = jnp.concatenate(
+        [
+            jnp.concatenate([value[: tall // 2], value[tall // 2 :]], axis=1),
+            jnp.concatenate([extra, extra], axis=1),
+            jnp.zeros((lines - tall // 2 - 8, columns), jnp.float32),
+        ],
+        axis=0,
+    ).reshape(small.shape)
+    late.run(0)
+
+    @pl.when(space > 0)
+    def _():
+        for n in range(PARTS):
+            grad_down(n).wait_send()
+            grad_up(n).wait_recv()
+
+    @pl.when(space < last)
+    def _():
+        for n in range(PARTS):
+            grad_up(n).wait_send()
+            grad_down(n).wait_recv()
+
+    rim(back_taps, glo, 0)
+    rim(back_taps, ghi, 1)
 
     @pl.loop(0, steps)
     def _(step):
-        for stage, at in BACKWARD_AT:
+        for stage, at in WIDE_AT:
 
             @pl.when(step == steps * at // 24)
             def _():
-                stages.run(stage)
+                wide.run(stage)
+
+        for stage, at in BACKWARD_AT:
+
+            @pl.when(step == steps * at // 24)
+            def _():
+                late.run(stage)
 
         row = step * STEP
-        cells = patch(taps, row)
-        res = jnp.dot(w[...], cells, preferred_element_type=jnp.float32)
+        res = jnp.dot(back_w[...], patch(back_taps, row), preferred_element_type=jnp.float32)
         for z in range(depth):
             for r in range(STEP):
                 out[z, row + r] = res[
-                    z * ins : (z + 1) * ins, r * columns : (r + 1) * columns
+                    z * channels : (z + 1) * channels, r * columns : (r + 1) * columns
                 ].astype(out.dtype)
 
-    stages.run(6)
+    wide.run(6)
+    late.run(6)
 
 
 def banded(w, depth):
@@ -271,22 +360,12 @@
     return jnp.concatenate(lines, axis=0)
 
 
-def neighbours(planes):
-    count = lax.axis_size("space")
-    up = [(i, i + 1) for i in range(count - 1)]
-    down = [(i + 1, i) for i in range(count - 1)]
-    lo = lax.ppermute(planes[-1], "space", up)
-    hi = lax.ppermute(planes[0], "space", down)
-    return lo, hi
-
-
 def local(volumes, kernel, bias, cotangent, finished_grads):
     volume = volumes[0].transpose(1, 2, 0, 3)
     cot = cotangent[0].transpose(1, 2, 0, 3)
     depth, rows, ins, columns = volume.shape
     outs = cot.shape[2]
     planes = depth + 2
-    lo, hi = neighbours(volume)
     forward_w = banded(kernel.transpose(0, 3, 1, 2, 4).reshape(3, outs, 9 * ins), depth)
     backward_w = banded(
         kernel[::-1, ::-1, ::-1].transpose(0, 4, 1, 2, 3).reshape(3, ins, 9 * outs), depth
@@ -303,44 +382,46 @@
     flat = jnp.pad(finished_grads.reshape(-1), (0, parts * columns * devices - entries))
     tall = 27 * ins // 2
     small_parts = share((tall + 8) * columns)
-    act, gp, small, summed = pl.pallas_call(
-        forward_kernel,
+    narrow = jnp.bfloat16
+    act, gvol, small_sum, summed = pl.pallas_call(
+        fused_kernel,
         out_shape=(
-            jax.ShapeDtypeStruct((depth, rows, outs, columns), jnp.bfloat16),
-            jax.ShapeDtypeStruct((depth, rows, outs, columns), jnp.bfloat16),
-            jax.ShapeDtypeStruct((small_parts * devices, columns), jnp.float32),
+            jax.ShapeDtypeStruct(cot.shape, narrow),
+            jax.ShapeDtypeStruct(volume.shape, narrow),
+            jax.ShapeDtypeStruct((*sizes, small_parts, columns), jnp.float32),
             jax.ShapeDtypeStruct((*sizes, parts, columns), jnp.float32),
         ),
-        in_specs=[VMEM] * 7,
+        in_specs=[VMEM] * 6,
         out_specs=(VMEM,) * 4,
         scratch_shapes=[
-            pltpu.VMEM((planes, rows + 2, 3 * ins, columns), jnp.bfloat16),
+            pltpu.VMEM((planes, rows + 2, 3 * ins, columns), narrow),
+            pltpu.VMEM((planes, rows + 2, 3 * outs, columns), narrow),
             pltpu.VMEM((planes * 9 * ins + 16, depth * outs), jnp.float32),
+            pltpu.VMEM(cot.shape, narrow),
+            pltpu.VMEM(volume.shape[1:], narrow),
+            pltpu.VMEM(volume.shape[1:], narrow),
+            pltpu.VMEM(cot.shape[1:], narrow),
+            pltpu.VMEM(cot.shape[1:], narrow),
+            pltpu.VMEM((*sizes, small_parts, columns), jnp.float32),
+            pltpu.SemaphoreType.DMA((2,)),
+            pltpu.SemaphoreType.DMA((2,)),
+            pltpu.SemaphoreType.DMA((2, PARTS)),
+            pltpu.SemaphoreType.DMA((2, PARTS)),
             *sum_scratch(parts, columns),
-        ],
-        compiler_params=pltpu.CompilerParams(
-            vmem_limit_bytes=48 * 2**20, collective_id=0, has_side_effects=True
-        ),
-        name="forward",
-    )(lo, volume, hi, forward_w, tall_bias, cot, flat.reshape(*sizes, parts, columns))
-    glo, ghi = neighbours(gp)
-    gvol, small_sum = pl.pallas_call(
-        backward_kernel,
-        out_shape=(
-            jax.ShapeDtypeStruct((depth, rows, ins, columns), jnp.bfloat16),
-            jax.ShapeDtypeStruct((*sizes, small_parts, columns), jnp.float32),
-        ),
-        in_specs=[VMEM] * 5,
-        out_specs=(VMEM,) * 2,
-        scratch_shapes=[
-            pltpu.VMEM((planes, rows + 2, 3 * outs, columns), jnp.bfloat16),
             *sum_scratch(small_parts, columns),
         ],
         compiler_params=pltpu.CompilerParams(
-            vmem_limit_bytes=48 * 2**20, collective_id=1, has_side_effects=True
+            vmem_limit_bytes=52 * 2**20, collective_id=0, has_side_effects=True
         ),
-        name="backward",
-    )(glo, gp, ghi, backward_w, small.reshape(*sizes, small_parts, columns))
+        name="fused",
+    )(
+        volume,
+        forward_w,
+        backward_w,
+        tall_bias,
+        cot,
+        flat.reshape(*sizes, parts, columns),
+    )
     count = lax.axis_size("dp") * lax.axis_size("space") * depth * rows * columns
     scale = 1.0 / math.sqrt(count)
     lines = small_sum.reshape(-1, columns)

time: 103 us -> 86.9 us (0.84)
  starting transfers between devices: 7.4 us -> 0 us
  local copies, waits for them, and re-layouts: 18 us -> 12.5 us
  waiting for transfers between devices: 1.55 us -> 0 us
    ppermute x4 -> x0, starting transfers between devices: 7.4 us -> none  [the longest x2 4.68 us: neighbours(): lo = lax.ppermute(planes[-1], 'space', up)]
    squeeze x2 -> x0, local copies, waits for them, and re-layouts: 4.06 us -> none  [neighbours(): hi = lax.ppermute(planes[0], 'space', down)]
    unnamed x33 -> x11, local copies, waits for them, and re-layouts: 11.2 us -> 8.74 us
    ppermute x4 -> x0, waiting for transfers between devices: 1.55 us -> none  [the longest x2 1.55 us: neighbours(): hi = lax.ppermute(planes[0], 'space', down)]
    pallas_call x2 -> x1, Pallas kernels: 72.8 us -> 71.9 us  [local(): pl.pallas_call(fused_kernel, out_shape=(jax.ShapeDtypeStruct(cot.shape, n...]
  transfers between devices with their start and end apart: 4 -> 0, of which waited for: 1 -> 0; matrix products, arithmetic and copies ran while one was open for 7% -> 0% of each run, Pallas kernels for 0% -> 0%
where the time goes in v2:
time: 86.9 us; the launch traced here: 86.6 us
  Pallas kernels  71.9 us (83%)
  local copies, waits for them, and re-layouts  12.5 us (14%)
  other arithmetic  1.53 us (2%)
    pallas_call x1, Pallas kernels, local(): pl.pallas_call(fused_kernel, out_shape=(jax.ShapeDtypeStruct(cot.shape, n...  71.9 us
    unnamed x11, local copies, waits for them, and re-layouts  8.74 us

profile of v2, /device:TPU:0, one launch (start us, length us, event | category | flops | bytes accessed | tf_op | source)
XLA Modules:
  0.0 86.6 jit_solution(9915033677557762465)
XLA Ops:
  0.6 0.7 tile.2
  1.3 0.1 broadcast_in_dim_tile.4.bias
  1.4 1.1 %copy.17 = bf16[3,64,288]{2,0,1:T(4,128)(2,1)S(1)} copy(bf16[3,64,288]{1,2,0:T(8,128)(2,1)} %bitcast.39) | data formatting | bytes 221184 | tf_op jit(solution)/shard_map/reshape | solution.py:369
  2.6 0.0 copy-start.2
  2.6 0.1 reshape.40
  2.7 0.1 fusion.5.w
  2.8 1.0 %reverse_bitcast_fusion = bf16[3,32,3,3,64]{4,1,3,2,0:T(8,128)(2,1)S(1)} fusion(bf16[3,3,3,64,32]{3,4,2,1,0:T(8,128)(2,1)} %param.6), kind=kLoop, calls=%fused_computation.13 | loop fusion | bytes 221184 | tf_op jit(solution)/shard_map/transpose | solution.py:371
  3.8 0.2 copy.18
  4.0 0.0 copy-start
  4.0 0.2 reshape.41
  4.2 0.1 copy.19
  4.3 0.1 reshape.42
  4.4 0.1 fusion.4.back_w
  4.5 0.0 copy-done.2
  4.5 1.2 %copy.27 = bf16[1,32,2,48,128]{4,1,3,2,0:T(8,128)(2,1)} copy(bf16[1,32,2,48,128]{4,3,2,1,0:T(8,128)(2,1)S(1)} %copy-done.2) | data formatting | bytes 1572864 | tf_op args[0]
  5.7 0.0 copy-done
  5.7 1.8 %copy.26 = bf16[1,64,2,48,128]{4,1,3,2,0:T(8,128)(2,1)} copy(bf16[1,64,2,48,128]{4,3,2,1,0:T(8,128)(2,1)S(1)} %copy-done) | data formatting | bytes 3145728 | tf_op args[3]
  7.5 71.9 %fused.1 = (bf16[2,48,64,128]{3,2,1,0:T(8,128)(2,1)}, bf16[2,48,32,128]{3,2,1,0:T(8,128)(2,1)S(1)}, f32[2,4,4,16,128]{4,3,2,1,0:T(8,128)S(1)}, f32[2,4,4,64,128]{4,3,2,1,0:T(8,128)}) custom-call(bf16[2,48,32,128]{3,2,1,0:T(8,128)(2,1)} %bitcast.35, bf16[128,1152]{1,0:T(8,128)(2,1)S(1)} %fusion.5.w, bf16[64,2304]{1,0:T(8,128)(2,1)S(1)} %fusion.4.back_w, ...), custom_call_target="tpu_custom_call" | custom-call | tf_op jit(solution)/shard_map/fused/pallas_call | solution.py:386
  79.4 3.6 %copy.22 = bf16[1,64,2,48,128]{4,3,2,1,0:T(8,128)(2,1)} copy(bf16[1,64,2,48,128]{4,1,3,2,0:T(8,128)(2,1)} %bitcast.36) | data formatting | bytes 3145728
  83.0 0.0 copy-start.1
  83.0 1.2 %copy.23 = bf16[1,32,2,48,128]{4,3,2,1,0:T(8,128)(2,1)} copy(bf16[1,32,2,48,128]{4,1,3,2,0:T(8,128)(2,1)S(1)} %bitcast.31) | data formatting | bytes 1572864
  84.2 0.5 fusion.6
  84.7 0.1 fusion.7
  84.8 0.8 maximum_multiply_fusion
  85.6 0.0 copy-done.1
  85.6 1.0 %copy.29 = f32[262144]{0:T(1024)} copy(f32[262144]{0:T(1024)S(1)} %bitcast.37) | data formatting | bytes 2097152
Async XLA Ops:
  2.6 2.0 %copy-start.2 = (bf16[1,32,2,48,128]{4,3,2,1,0:T(8,128)(2,1)S(1)}, bf16[1,32,2,48,128]{4,3,2,1,0:T(8,128)(2,1)}, u32[]{:S(2)}) copy-start(bf16[1,32,2,48,128]{4,3,2,1,0:T(8,128)(2,1)} %param.5) | copy-start | bytes 2359300
  4.0 1.8 %copy-start = (bf16[1,64,2,48,128]{4,3,2,1,0:T(8,128)(2,1)S(1)}, bf16[1,64,2,48,128]{4,3,2,1,0:T(8,128)(2,1)}, u32[]{:S(2)}) copy-start(bf16[1,64,2,48,128]{4,3,2,1,0:T(8,128)(2,1)} %param.8) | copy-start | bytes 4718596
  83.0 2.6 %copy-start.1 = (f32[2,4,4,64,128]{4,3,2,1,0:T(8,128)S(1)}, f32[2,4,4,64,128]{4,3,2,1,0:T(8,128)}, u32[]{:S(2)}) copy-start(f32[2,4,4,64,128]{4,3,2,1,0:T(8,128)} %get-tuple-element.12) | copy-start | bytes 3145732

commit v3 on v2

--- a/solution.py
+++ b/solution.py
@@ -9,7 +9,7 @@
 from jax.sharding import PartitionSpec as P
 
 VMEM = pl.BlockSpec(memory_space=pltpu.VMEM)
-STEP = 2
+STEP = 4
 PARTS = 4
 FORWARD_AT = ((1, 1), (2, 11), (3, 16), (4, 20))
 WIDE_AT = ((5, 6),)
@@ -219,7 +219,7 @@
     clear_rim(taps)
     clear_rim(back_taps)
 
-    @pl.loop(0, rows)
+    @pl.loop(0, rows, unroll=8)
     def _(row):
         for z in range(depth):
             fill(taps, z + 1, row, mid[z, row])
@@ -229,7 +229,7 @@
         def _():
             plane_in[...] = jnp.zeros_like(plane_in)
 
-        @pl.loop(0, rows)
+        @pl.loop(0, rows, unroll=8)
         def _(row):
             fill(target, depth + 1 if edge else 0, row, plane_in[row])
 

time: 86.9 us -> 70.3 us (0.81)
  Pallas kernels: 71.9 us -> 55.3 us
    pallas_call x1, Pallas kernels: 71.9 us -> 55.3 us  [local(): pl.pallas_call(fused_kernel, out_shape=(jax.ShapeDtypeStruct(cot.shape, n...]
where the time goes in v3:
time: 70.3 us; the launch traced here: 70 us
  Pallas kernels  55.3 us (79%)
  local copies, waits for them, and re-layouts  12.5 us (18%)
  other arithmetic  1.53 us (2%)
  between operations  0.74 us (1%)
    pallas_call x1, Pallas kernels, local(): pl.pallas_call(fused_kernel, out_shape=(jax.ShapeDtypeStruct(cot.shape, n...  55.3 us
    unnamed x11, local copies, waits for them, and re-layouts  8.74 us

profile of v3, /device:TPU:0, one launch (start us, length us, event | category | flops | bytes accessed | tf_op | source)
XLA Modules:
  0.0 70.0 jit_solution(10238558148566760219)
XLA Ops:
  0.6 0.7 tile.2
  1.3 0.1 broadcast_in_dim_tile.4.bias
  1.4 1.1 %copy.17 = bf16[3,64,288]{2,0,1:T(4,128)(2,1)S(1)} copy(bf16[3,64,288]{1,2,0:T(8,128)(2,1)} %bitcast.39) | data formatting | bytes 221184 | tf_op jit(solution)/shard_map/reshape | solution.py:369
  2.6 0.0 copy-start.2
  2.6 0.1 reshape.40
  2.7 0.1 fusion.5.w
  2.8 1.0 %reverse_bitcast_fusion = bf16[3,32,3,3,64]{4,1,3,2,0:T(8,128)(2,1)S(1)} fusion(bf16[3,3,3,64,32]{3,4,2,1,0:T(8,128)(2,1)} %param.6), kind=kLoop, calls=%fused_computation.13 | loop fusion | bytes 221184 | tf_op jit(solution)/shard_map/transpose | solution.py:371
  3.8 0.2 copy.18
  4.0 0.0 copy-start
  4.0 0.2 reshape.41
  4.2 0.1 copy.19
  4.3 0.1 reshape.42
  4.4 0.1 fusion.4.back_w
  4.5 0.0 copy-done.2
  4.5 1.2 %copy.27 = bf16[1,32,2,48,128]{4,1,3,2,0:T(8,128)(2,1)} copy(bf16[1,32,2,48,128]{4,3,2,1,0:T(8,128)(2,1)S(1)} %copy-done.2) | data formatting | bytes 1572864 | tf_op args[0]
  5.7 0.0 copy-done
  5.7 1.8 %copy.26 = bf16[1,64,2,48,128]{4,1,3,2,0:T(8,128)(2,1)} copy(bf16[1,64,2,48,128]{4,3,2,1,0:T(8,128)(2,1)S(1)} %copy-done) | data formatting | bytes 3145728 | tf_op args[3]
  7.5 55.3 %fused.1 = (bf16[2,48,64,128]{3,2,1,0:T(8,128)(2,1)}, bf16[2,48,32,128]{3,2,1,0:T(8,128)(2,1)S(1)}, f32[2,4,4,16,128]{4,3,2,1,0:T(8,128)S(1)}, f32[2,4,4,64,128]{4,3,2,1,0:T(8,128)}) custom-call(bf16[2,48,32,128]{3,2,1,0:T(8,128)(2,1)} %bitcast.35, bf16[128,1152]{1,0:T(8,128)(2,1)S(1)} %fusion.5.w, bf16[64,2304]{1,0:T(8,128)(2,1)S(1)} %fusion.4.back_w, ...), custom_call_target="tpu_custom_call" | custom-call | tf_op jit(solution)/shard_map/fused/pallas_call | solution.py:386
  62.8 3.6 %copy.22 = bf16[1,64,2,48,128]{4,3,2,1,0:T(8,128)(2,1)} copy(bf16[1,64,2,48,128]{4,1,3,2,0:T(8,128)(2,1)} %bitcast.36) | data formatting | bytes 3145728
  66.4 0.0 copy-start.1
  66.4 1.2 %copy.23 = bf16[1,32,2,48,128]{4,3,2,1,0:T(8,128)(2,1)} copy(bf16[1,32,2,48,128]{4,1,3,2,0:T(8,128)(2,1)S(1)} %bitcast.31) | data formatting | bytes 1572864
  67.6 0.5 fusion.6
  68.1 0.1 fusion.7
  68.2 0.8 %maximum_multiply_fusion = f32[864,64]{1,0:T(8,128)} fusion(f32[432,64]{1,0:T(8,128)S(1)} %get-tuple-element.24, f32[432,64]{1,0:T(8,128)S(1)} %get-tuple-element.23), kind=kLoop, calls=%fused_computation.10 | loop fusion | flops 110592 | bytes 442368 | tf_op jit(solution)/shard_map/mul | solution.py:435
  69.0 0.0 copy-done.1
  69.0 1.0 %copy.29 = f32[262144]{0:T(1024)} copy(f32[262144]{0:T(1024)S(1)} %bitcast.37) | data formatting | bytes 2097152
Async XLA Ops:
  2.6 2.0 %copy-start.2 = (bf16[1,32,2,48,128]{4,3,2,1,0:T(8,128)(2,1)S(1)}, bf16[1,32,2,48,128]{4,3,2,1,0:T(8,128)(2,1)}, u32[]{:S(2)}) copy-start(bf16[1,32,2,48,128]{4,3,2,1,0:T(8,128)(2,1)} %param.5) | copy-start | bytes 2359300
  4.0 1.8 %copy-start = (bf16[1,64,2,48,128]{4,3,2,1,0:T(8,128)(2,1)S(1)}, bf16[1,64,2,48,128]{4,3,2,1,0:T(8,128)(2,1)}, u32[]{:S(2)}) copy-start(bf16[1,64,2,48,128]{4,3,2,1,0:T(8,128)(2,1)} %param.8) | copy-start | bytes 4718596
  66.4 2.6 %copy-start.1 = (f32[2,4,4,64,128]{4,3,2,1,0:T(8,128)S(1)}, f32[2,4,4,64,128]{4,3,2,1,0:T(8,128)}, u32[]{:S(2)}) copy-start(f32[2,4,4,64,128]{4,3,2,1,0:T(8,128)} %get-tuple-element.12) | copy-start | bytes 3145732
